TPU v7x, 128 devices: a whole 4x4x4 slice. The times are simulated.
128 devices in a mesh: tm: 8 (over y, core), space: 16 (over z, x).
Axes of the slice: x: 4, y: 4, z: 4, core: 2. Of those that a mesh axis runs over, the one named last changes fastest.
Arguments:
- vorticity: float32 [512, 8192], P('space'), may hold values from -6 to 6
- stream: float32 [512, 8192], P('space'), may hold values from -0.8 to 0.8
- forcing: float32 [512, 8192], P('space'), may hold values from -1.2 to 1.2, as said below
- conv_in: float32 [8, 3, 3], replicated, may hold values from -2 to 2
- conv_out: float32 [8, 3, 3], replicated, may hold values from -0.75 to 0.75
Outputs:
- slice_ends: float32 [8, 512, 8192], P('tm', 'space')
Inputs may be any that keep to these rules, and one draw needn't show every extreme that they name: `forcing`: a vorticity source field.
All inputs are finite; a program needn't handle non-finite values.
Results may differ from a plain program's by a relative error of at most 0.0001.
Values sent between devices are 32-bit elements; how exact they have to be, the bound alone decides.
A program may use at most 128 MiB of HBM per device.

v0:
```python
import functools
import math

import jax
import jax.numpy as jnp
import numpy as np
from jax import lax
from jax.experimental import pallas as pl
from jax.experimental.pallas import tpu as pltpu
from jax.sharding import PartitionSpec as P

F32 = jnp.float32
VMEM = pltpu.VMEM
MESH = pl.DeviceIdType.MESH
HIGH = lax.Precision.HIGHEST

STEPS = 4
SLICES = 8
LANES = 128
CHUNK = 64
INNER = 32
HALO = 16
PAD = 8
TALL = INNER + 2 * HALO + 2 * PAD
OWN = PAD + HALO
PITCH = 33
BLOCKS = 16
REACH = 28
WINDOW = 2 * REACH


def fine_weights():
    shift = np.polynomial.Polynomial([-0.45, 0.2])
    of_w = sum(shift**j / math.factorial(j) for j in range(5))
    of_f = sum(shift**j / math.factorial(j + 1) for j in range(4))
    return [float(v) for v in of_w.coef], [float(v) for v in of_f.coef] + [0.0]


def lane_iota():
    return lax.broadcasted_iota(jnp.int32, (8, LANES), 1)


def lane_shifted(value, up):
    lane = lax.broadcasted_iota(jnp.int32, value.shape, 2)
    if up:
        rolled = pltpu.roll(value, LANES - 1, 2)
        return jnp.where(lane == LANES - 1, jnp.concatenate([rolled[1:], rolled[:1]], axis=0), rolled)
    rolled = pltpu.roll(value, 1, 2)
    return jnp.where(lane == 0, jnp.concatenate([rolled[-1:], rolled[:-1]], axis=0), rolled)


def lane_gather(value, index):
    return jnp.take_along_axis(value, index, axis=1)


def next_chunk():
    lane = lane_iota()
    return jnp.where(lane < 64, lane + 64, jnp.where(lane == 127, 0, lane - 63))


def previous_chunk():
    lane = lane_iota()
    return jnp.where(lane >= 64, lane - 64, jnp.where(lane == 0, 127, lane + 63))


def swap_tiles_and_lanes(tiles):
    lane = lane_iota()
    for bit in range(4):
        width = 4 << bit
        high = (lane // width) % 2 == 1
        out = list(tiles)
        for m in range(16):
            if not m >> bit & 1:
                a, b = tiles[m], tiles[m | 1 << bit]
                out[m] = jnp.where(high, pltpu.roll(b, width, 1), a)
                out[m | 1 << bit] = jnp.where(high, b, pltpu.roll(a, LANES - width, 1))
        tiles = out
    return tiles


def to_chunks(tiles):
    lane = lane_iota()
    index = ((lane % 4) * 2 + lane // 64) * 16 + (lane % 64) // 4
    return swap_tiles_and_lanes([lane_gather(t, index) for t in tiles])


def from_chunks(tiles):
    lane = lane_iota()
    block = lane // 16
    index = (block % 2) * 64 + (lane % 16) * 4 + block // 2
    return [lane_gather(t, index) for t in swap_tiles_and_lanes(tiles)]


def coarse_step(count, w_in, w_out, win, values, extra, taps, sums, parts):
    lanes = win.shape[0]
    off = REACH - 4 * count
    at = [pl.ds(off + q, 8, stride=count) for q in range(count)]

    def tiles(q):
        return slice(lanes * q, lanes * q + lanes)

    for q in range(count):
        x = win[:, at[q], :]
        for dx, v in enumerate((lane_shifted(x, False), x, lane_shifted(x, True))):
            for dy in range(3):
                place = q + 1 - dy
                if place < 0:
                    taps[dy * 3 + dx, tiles(count - 1)] = pltpu.roll(v, 7, 1)
                elif place >= count:
                    taps[dy * 3 + dx, tiles(0)] = pltpu.roll(v, 1, 1)
                else:
                    taps[dy * 3 + dx, tiles(place)] = v
    total = lanes * count
    group = GROUP

    def few(i, _):
        some = pl.ds(jnp.minimum(i * group, total - group), group)
        x = taps[:, some]
        acc = None
        for h in range(8):
            hidden = jnp.tanh(jnp.sum(w_in[h][:, None] * x, axis=0))
            term = w_out[h][:, None] * hidden[None]
            acc = term if acc is None else acc + term
        sums[:, some] = acc
        return 0

    lax.fori_loop(0, -(-total // group), few, 0)
    for q in range(count):
        for dy in range(3):
            low = lane_shifted(sums[dy * 3, tiles(q)], False)
            high = lane_shifted(sums[dy * 3 + 2, tiles(q)], True)
            v = low + high + sums[dy * 3 + 1, tiles(q)]
            parts[dy, q + 1] = v
            if q == 0 and dy == 2:
                parts[dy, count + 1] = pltpu.roll(v, 7, 1)
            if q == count - 1 and dy == 0:
                parts[dy, 0] = pltpu.roll(v, 1, 1)
    for q in range(count):
        g = win[:, at[q], :] + (parts[0, q] + parts[1, q + 1] + parts[2, q + 2])
        values[:, at[q], :] = g
        if extra is not None:
            win[:, at[q], :] = g + extra(off + q, count)


def own_columns(value):
    rolled = pltpu.roll(value, 64, 2)
    lane = lax.broadcasted_iota(jnp.int32, (2, 8, LANES), 2)
    return jnp.where(lane < 64, rolled[:2], rolled[1:])


def fine_stage(src, dst, base, pcoef, qcoef, force, off, count, scale, of_base):
    at = [pl.ds(off + q, 8, stride=count) for q in range(-1, count + 1)]

    def block(first, size):
        centre = pl.ds(first, size)
        wide = [src[pl.ds(first - 1, size + 2), a, :] for a in at[1:-1]]
        column = [src[centre, at[0], :]] + [x[1:-1] for x in wide] + [src[centre, at[-1], :]]
        results = []
        for q in range(count):
            slot = (centre, at[q + 1], slice(None))
            left, right = wide[q][:-2], wide[q][2:]
            above, below = column[q + 2], column[q]
            t = pcoef[slot] * (right - left) + qcoef[slot] * (above - below) + (left + below)
            if scale != 1.0:
                t = scale * t
            here = column[q + 1] if src is base else base[slot]
            t = t + (of_base * here + force[slot])
            dst[slot] = t
            results.append(t)
        return results

    group = 10
    last = block(CHUNK - 1, 2)
    first = block(1, 2)
    block(3, group)
    ahead, back = next_chunk(), previous_chunk()
    for q in range(count):
        dst[0, at[q + 1], :] = lane_gather(last[q][1], back)
        dst[CHUNK + 1, at[q + 1], :] = lane_gather(first[q][0], ahead)

    def body(g, _):
        block(3 + g * group, group)
        return 0

    lax.fori_loop(1, (CHUNK - 4) // group, body, 0)


def fine_run(state, one, two, pcoef, qcoef, force):
    of_w, _ = fine_weights()
    for step in range(STEPS):
        count = 9 if step == 0 else 8 - step
        off = 4 if step == 0 else PAD + 4 * step
        shared = (state, pcoef, qcoef)
        fine_stage(state, one, *shared, force.at[3], off, count, 1.0, of_w[3] / of_w[4])
        fine_stage(one, two, *shared, force.at[2], off, count, 1.0, of_w[2] / of_w[4])
        fine_stage(two, one, *shared, force.at[1], off, count, 1.0, of_w[1] / of_w[4])
        fine_stage(one, state, *shared, force.at[0], PAD + 4 * step + 4, 7 - step, of_w[4], of_w[0])


def ghosts(ref):
    ahead, back = next_chunk(), previous_chunk()
    for r in range(PAD, TALL - PAD, 8):
        ref[0, r : r + 8, :] = lane_gather(ref[CHUNK, r : r + 8, :], back)
        ref[CHUNK + 1, r : r + 8, :] = lane_gather(ref[1, r : r + 8, :], ahead)


def coefficients(stream, forcing, pcoef, qcoef, force):
    of_w, of_f = fine_weights()
    ghosts(stream)
    count = 9
    at = [pl.ds(4 + q, 8, stride=count) for q in range(-1, count + 1)]

    group = 4

    def body(g, _):
        first = 1 + g * group
        c = pl.ds(first, group)
        wide = [stream[pl.ds(first - 1, group + 2), a, :] for a in at[1:-1]]
        x = [stream[c, at[0], :]] + [v[1:-1] for v in wide] + [stream[c, at[-1], :]]
        for q in range(count):
            a = at[q + 1]
            pcoef[c, a, :] = 0.5 - 1.25 * (x[q + 2] - x[q])
            qcoef[c, a, :] = 0.5 + 1.25 * (wide[q][2:] - wide[q][:-2])
            f = forcing[c, a, :]
            force[0, c, a, :] = of_f[0] * f
            for k in range(1, 4):
                force[k, c, a, :] = (of_f[k] / of_w[4]) * f
        return 0

    lax.fori_loop(0, CHUNK // group, body, 0)


def natural_to_rows(source, nat):
    for c in range(64):
        nat[c * PITCH : c * PITCH + INNER, :] = source[:, c * LANES : (c + 1) * LANES]


def rows_to_chunks(nat, lam):
    low = lax.broadcasted_iota(jnp.int32, (64, LANES), 1) < 64
    for i in range(INNER // 2):
        j = i + INNER // 2
        at_i, at_j = pl.ds(i, 64, stride=PITCH), pl.ds(j, 64, stride=PITCH)
        flipped = jnp.concatenate([nat[at_i, :], nat[at_j, :]], axis=0).T
        top, bottom = flipped[:64], flipped[64:]
        lam[at_i, :] = jnp.where(low, top, pltpu.roll(bottom, 64, 1))
        lam[at_j, :] = jnp.where(low, pltpu.roll(top, 64, 1), bottom)


def chunks_to_rows(lam, nat):
    low = lax.broadcasted_iota(jnp.int32, (64, LANES), 1) < 64
    for i in range(INNER // 2):
        j = i + INNER // 2
        at_i, at_j = pl.ds(i, 64, stride=PITCH), pl.ds(j, 64, stride=PITCH)
        x, y = lam[at_i, :], lam[at_j, :]
        top = jnp.where(low, x, pltpu.roll(y, 64, 1))
        bottom = jnp.where(low, pltpu.roll(x, 64, 1), y)
        flipped = jnp.concatenate([top, bottom], axis=0).T
        nat[at_i, :] = flipped[:64]
        nat[at_j, :] = flipped[64:]


def store_own(lam, ref):
    for c in range(CHUNK):
        ref[1 + c, OWN : OWN + INNER, :] = lam[c * PITCH : c * PITCH + INNER, :]


def load_own(ref, lam):
    for c in range(CHUNK):
        lam[c * PITCH : c * PITCH + INNER, :] = ref[1 + c, OWN : OWN + INNER, :]


def spaced_tiles(tiles, rolled):
    lane = lane_iota()
    turned = [pltpu.roll(t, 64, 1) for t in tiles]
    for k in range(BLOCKS):
        v = jnp.where(lane < 64, turned[k - 1], turned[k])
        rolled[k] = v
        if k < 2:
            rolled[BLOCKS + k] = v


def block_means(state):
    tiles = []
    for m in range(BLOCKS):
        four = [state[1 + 4 * m : 5 + 4 * m, pl.ds(OWN + q, 8, stride=4), :] for q in range(4)]
        tiles.append(0.0625 * jnp.sum((four[0] + four[1]) + (four[2] + four[3]), axis=0))
    return from_chunks(tiles)


def coarse_in_chunks(pieces, coarse):
    for half in range(2):
        at = pl.ds(half, 8, stride=2)
        tiles = to_chunks([pieces[m // 2, m % 2, at, :] for m in range(BLOCKS)])
        for m in range(BLOCKS):
            coarse[m, at, :] = tiles[m]


def spread_coarse(coarse, base, state):
    upper = lax.broadcasted_iota(jnp.int32, (8, LANES), 0) < 4

    def body(m, _):
        c = pl.ds(4 * m, 4)
        for r in range(8):
            v = jnp.where(upper, coarse[m, 2 * r : 2 * r + 1, :], coarse[m, 2 * r + 1 : 2 * r + 2, :])[None]
            old = base(c, r)
            v = jnp.broadcast_to(v, (4, 8, LANES)) if old is None else old + v
            state[pl.ds(4 * m + 1, 4), PAD + 8 * r : PAD + 8 * r + 8, :] = v
        return 0

    lax.fori_loop(0, BLOCKS, body, 0)


GROUP = 3
AHEAD = 24
FIRST_PART, SECOND_PART = 1, 4


def kernel(
    conv_in, conv_out, vort_hbm, stream_hbm, force_hbm, out, delta_out,
    inputs, nat, lam, fields, state, one, two, pcoef, qcoef, force,
    start, win, old, new, taps, sums, parts, w_in, w_out,
    rolled, means, sent, got, edge, coarse, packed,
    in_sem, send_sem, recv_sem,
):
    t, z = lax.axis_index("tm"), lax.axis_index("space")
    slabs = lax.axis_size("space")
    parity = lax.rem(t, 2)
    used = [0]

    def slot_of(k):
        return lax.rem(t + k, SLICES)

    def slab_of(d):
        return lax.rem(z + d + slabs, slabs)

    def reserve(count):
        used[0] += count
        return used[0] - count

    def remote(src, dst, to, send=None, recv=None):
        if send is None:
            send = recv = reserve(1)
        return pltpu.make_async_remote_copy(
            src_ref=src, dst_ref=dst, send_sem=send_sem.at[send], recv_sem=recv_sem.at[recv],
            device_id=to, device_id_type=MESH,
        )

    def start_all(copies):
        for c in copies:
            c.start()

    def recv_all(copies):
        for c in copies:
            c.wait_recv()

    def sent_all(copies):
        for c in copies:
            c.wait_send()

    loads = [
        pltpu.make_async_copy(ref, inputs.at[i], in_sem.at[i])
        for i, ref in enumerate((vort_hbm, stream_hbm, force_hbm))
    ]
    start_all(loads)
    barrier = pltpu.get_barrier_semaphore()
    peers = [(slot_of(k), z) for k in range(1, SLICES)] + [(t, slab_of(d)) for d in (-3, -2, -1, 1, 2, 3)]
    for p in peers:
        pl.semaphore_signal(barrier, inc=1, device_id=p, device_id_type=MESH)
    for dy in range(3):
        v_in, v_out = conv_in[dy], 0.5 * conv_out[dy]
        for dx in range(3):
            for h in range(8):
                w_in[h, dy * 3 + dx] = jnp.broadcast_to(v_in[dx : dx + 1, h : h + 1], (8, LANES))
                w_out[h, dy * 3 + dx] = jnp.broadcast_to(v_out[dx : dx + 1, h : h + 1], (8, LANES))

    loads[0].wait()
    natural_to_rows(inputs.at[0], nat)
    for c in range(64):
        four = [nat[pl.ds(c * PITCH + q, 8, stride=4), :] for q in range(4)]
        m, k = c // 4, c % 4
        packed[m * 8 : m * 8 + 8, k * LANES : (k + 1) * LANES] = (four[0] + four[1]) + (four[2] + four[3])
    averages = jnp.where(
        lax.broadcasted_iota(jnp.int32, (4 * LANES, LANES), 0) // 4
        == lax.broadcasted_iota(jnp.int32, (4 * LANES, LANES), 1), 0.0625, 0.0,
    ).astype(F32)
    first = jnp.dot(packed[...], averages, precision=HIGH, preferred_element_type=F32)
    spaced_tiles([first[m * 8 : m * 8 + 8] for m in range(BLOCKS)], rolled.at[0])
    mine = pl.ds(2 * t, 3)
    near = [
        remote(rolled.at[0, mine], start.at[:, REACH - 4 - 8 * d : REACH + 4 - 8 * d, :], (t, slab_of(d)))
        for d in (-1, 1, -2, 2, -3, 3)
    ]

    @pl.when(t == 1)
    def _():
        rows_to_chunks(nat, lam)
        store_own(lam, state)

    inside = slice(1, CHUNK + 1)
    low, high = slice(OWN - HALO, OWN), slice(OWN + INNER, OWN + INNER + HALO)
    first_rows, last_rows = slice(OWN, OWN + HALO), slice(OWN + INNER - HALO, OWN + INNER)
    sibling = (t + 1 - 2 * parity, z)
    half = lax.rem(t // 2, 2)
    size = CHUNK // 4

    def part_of(which, part):
        return pl.ds(1 + 2 * size * which + size * part, size)

    across, helped, shared = [], [], [[], []]
    for part in range(2):
        some = part_of(half, part)
        across.append(
            [
                remote(fields.at[parity, some, last_rows], fields.at[parity, some, low], (t, slab_of(1))),
                remote(fields.at[parity, some, first_rows], fields.at[parity, some, high], (t, slab_of(-1))),
            ]
        )
        helped.append(
            [
                remote(fields.at[parity, some, rows], fields.at[parity, some, rows], (slot_of(k), z))
                for rows, k in ((low, SLICES - 2), (high, 2))
            ]
        )
        for k, which in enumerate((half, 1 - half)):
            some = part_of(which, part)
            shared[k].append(
                [remote(fields.at[parity, some, rows], fields.at[parity, some, rows], sibling) for rows in (low, high)]
            )
    early = [
        remote(state.at[inside, last_rows], state.at[inside, low], (t, slab_of(1))),
        remote(state.at[inside, first_rows], state.at[inside, high], (t, slab_of(-1))),
    ]
    loads[1].wait()
    loads[2].wait()

    def lay_out(which):
        natural_to_rows(inputs.at[1 + which], nat)
        rows_to_chunks(nat, lam)
        store_own(lam, fields.at[which])

    lay_out(parity)
    pl.semaphore_wait(barrier, len(peers))
    start_all(near)

    start_all(across[0])
    start_all(across[1])

    @pl.when(t == 1)
    def _():
        start_all(early)

    start[:, REACH - 4 : REACH + 4, :] = rolled[0, mine]
    lay_out(1 - parity)

    recv_all(near)
    win[...] = start[...]
    scratch = (taps, sums, parts)

    def rows_of(ref):
        return lambda r: ref[:, r : r + 8, :]

    def change(a, b):
        return lambda r: a[:, r : r + 8, :] - b[:, r : r + 8, :]

    def deliverer(phase, rows):
        send, recv = reserve(SLICES), reserve(SLICES)
        here = slice(0, rows)

        def copy(n, to, source):
            return remote(
                sent.at[phase, n, :, here], got.at[phase, source, :, here], (to, z), send + n, recv + source
            )

        def put(n, to, read):
            for r in range(0, rows, 8):
                sent[phase, n, :, r : r + 8, :] = own_columns(read(REACH - rows // 2 + r))

            @pl.when(t != to)
            def _():
                copy(n, to, t).start()

            @pl.when(t == to)
            def _():
                got[phase, t, :, here, :] = sent[phase, n, :, here, :]

        def take():
            @pl.when(t > 1)
            def _():
                for k in range(1, SLICES):
                    copy(2, 2, slot_of(k)).wait_recv()

        def done(pairs):
            for n, to in pairs:
                @pl.when(t != to)
                def _():
                    copy(n, to, t).wait_send()

        return put, take, done

    plain = lambda row, count: 0.0
    put_0, take_0, done_0 = deliverer(0, 16)
    for n in range(8):
        coarse_step(-(-(44 - 4 * n) // 8), w_in, w_out, win, old.at[n], plain if n < 7 else None, *scratch)
        if n < 6:
            put_0(n + 1, n + 2, rows_of(win))
        if n == FIRST_PART or n == SECOND_PART:
            part = int(n == SECOND_PART)
            recv_all(across[part])
            start_all(helped[part])
            start_all(shared[0][part])
        if n >= 6:
            recv_all(helped[n - 6])
            start_all(shared[1][n - 6])

    take_0()

    @pl.when(t > 1)
    def _():
        coarse_in_chunks(got.at[0], coarse)
        spread_coarse(coarse, lambda c, r: None, state)

    for copies in shared:
        for part in range(2):
            recv_all(copies[part])
    coefficients(fields.at[0], fields.at[1], pcoef, qcoef, force)

    @pl.when(t == 1)
    def _():
        recv_all(early)
        sent_all(early)

    @pl.when(t > 0)
    def _():
        ghosts(state)
        fine_run(state, one, two, pcoef, qcoef, force)

    def sharer(phase, shift, wanted, wanted_two):
        place = lax.rem(t + shift, SLICES)
        middle = slice(16, 24)
        send, recv, around = reserve(SLICES), reserve(SLICES), reserve(4 * SLICES)

        def copy(k, slot):
            return remote(
                rolled.at[phase + 1, pl.ds(2 * slot_of(k), 3)], means.at[phase, slot, :, middle],
                (slot_of(k), z), send + k, recv + slot,
            )

        def spread(n):
            return [
                remote(
                    means.at[phase, n, :, middle], means.at[phase, n, :, 16 - 8 * d : 24 - 8 * d],
                    (t, slab_of(d)), around + 4 * n + j, around + 4 * n + j,
                )
                for j, d in enumerate((-1, 1, -2, 2))
                if abs(d) == 1 or n in wanted_two
            ]

        has_slice = functools.reduce(jnp.logical_or, [place == n for n in wanted])

        def go():
            @pl.when(has_slice)
            def _():
                spaced_tiles(block_means(state), rolled.at[phase + 1])
                for k in range(1, SLICES):
                    copy(k, place).start()
                means[phase, place, :, middle, :] = rolled[phase + 1, pl.ds(2 * t, 3)]

        def pass_on():
            for n in wanted:
                @pl.when(place != n)
                def _():
                    copy(1, n).wait_recv()

                start_all(spread(n))

        def take(n):
            recv_all(spread(n))

        def done():
            @pl.when(has_slice)
            def _():
                for k in range(1, SLICES):
                    copy(k, place).wait_send()

            for n in wanted:
                sent_all(spread(n))

        return go, pass_on, take, done

    go_1, pass_1, arrived_1, shared_1 = sharer(0, SLICES - 1, range(0, 7), range(0, 4))
    go_1()
    copy_f = remote(state.at[inside, slice(OWN, OWN + INNER)], one.at[inside, slice(OWN, OWN + INNER)], (0, z))

    @pl.when(t == 1)
    def _():
        copy_f.start()

    bulk = [
        remote(state.at[1 + a : 1 + b, rows], edge.at[side, a:b], (t, slab_of(1 - 2 * side)))
        for a, b in ((0, AHEAD), (AHEAD, CHUNK))
        for side, rows in enumerate((last_rows, first_rows))
    ]

    @pl.when(t > 0)
    def _():
        start_all(bulk[:2])

    pass_1()

    @pl.when(t > 0)
    def _():
        start_all(bulk[2:])

    def corrected(phase, n, before):
        def extra(row, count):
            there = pl.ds(row - 8, 8, stride=count)
            return means[phase, n, :, there, :] - before[n, :, pl.ds(row, 8, stride=count), :]

        return extra

    put_1, take_1, done_1 = deliverer(1, 16)
    arrived_1(0)
    win[:, 8:48, :] = means[0, 0]
    for n in range(1, 8):
        if n < 7:
            arrived_1(n)
        coarse_step(
            -(-(44 - 4 * n) // 8), w_in, w_out, win, new.at[n], corrected(0, n, old) if n < 7 else None, *scratch
        )
        if n < 7:
            put_1(n, n + 1, change(new.at[n], old.at[n]))

    take_1()

    @pl.when(t == 1)
    def _():
        copy_f.wait_send()
        got[1] = jnp.zeros(got.shape[1:], F32)

    @pl.when(t > 0)
    def _():
        recv_all(bulk)
        sent_all(bulk)
        coarse_in_chunks(got.at[1], coarse)

        def base(c, r):
            if r < 2:
                return edge[0, c, 8 * r : 8 * r + 8, :]
            if r >= 6:
                return edge[1, c, 8 * (r - 6) : 8 * (r - 6) + 8, :]
            return state[pl.ds(c.start + 1, 4), PAD + 8 * r : PAD + 8 * r + 8, :]

        spread_coarse(coarse, base, state)
        ghosts(state)
        fine_run(state, one, two, pcoef, qcoef, force)

    go_2, pass_2, arrived_2, shared_2 = sharer(1, 0, range(1, 7), range(1, 3))
    go_2()
    pass_2()

    @pl.when(t == 0)
    def _():
        copy_f.wait_recv()
        load_own(one, lam)

    @pl.when(t > 0)
    def _():
        load_own(state, lam)

    put_2, take_2, done_2 = deliverer(2, 8)
    arrived_2(1)
    win[:, 8:48, :] = means[1, 1]
    for n in range(2, 8):
        if n < 7:
            arrived_2(n)
        coarse_step(
            -(-(40 - 4 * n) // 8), w_in, w_out, win, old.at[n], corrected(1, n, new) if n < 7 else None, *scratch
        )
        put_2(n, n, change(old.at[n], new.at[n]))

    chunks_to_rows(lam, nat)
    for c in range(64):
        inputs[0, :, c * LANES : (c + 1) * LANES] = nat[c * PITCH : c * PITCH + INNER, :]
    store = pltpu.make_async_copy(inputs.at[0], out, in_sem.at[0])
    store.start()

    @pl.when(t <= 1)
    def _():
        got[2] = jnp.zeros(got.shape[1:], F32)

    sent_all(near)
    for part in range(2):
        sent_all(across[part])
        sent_all(helped[part])
        sent_all(shared[0][part])
        sent_all(shared[1][part])
    done_0([(n, n + 1) for n in range(1, 7)])
    done_1([(n, n + 1) for n in range(1, 7)])
    done_2([(n, n) for n in range(2, 8)])
    shared_1()
    shared_2()
    take_2()
    for m in range(BLOCKS):
        delta_out[m * 8 : m * 8 + 8, :] = got[2, m // 2, m % 2, 0:8, :]
    store.wait()


def finish_kernel(fine, delta, out):
    copies = jnp.where(
        lax.broadcasted_iota(jnp.int32, (LANES, 4 * LANES), 0)
        == lax.broadcasted_iota(jnp.int32, (LANES, 4 * LANES), 1) // 4, 1.0, 0.0,
    ).astype(F32)
    wide = jnp.dot(delta[...], copies, precision=HIGH, preferred_element_type=F32)
    upper = lax.broadcasted_iota(jnp.int32, (8, 4 * LANES), 0) < 4
    for m in range(delta.shape[0] // 8):
        cols = slice(m * 4 * LANES, (m + 1) * 4 * LANES)
        for a in range(INNER // 8):
            r = m * 8 + 2 * a
            v = jnp.where(upper, wide[r : r + 1], wide[r + 1 : r + 2])
            out[0, a * 8 : a * 8 + 8, cols] = fine[a * 8 : a * 8 + 8, cols] + v


def body(vorticity, stream, forcing, conv_in, conv_out):
    rows, cols = vorticity.shape
    whole = (CHUNK + 2, TALL, LANES)
    vmem = pl.BlockSpec(memory_space=VMEM)
    anywhere = pl.BlockSpec(memory_space=pl.ANY)
    window = (3, WINDOW, LANES)
    shapes = [
        (3, rows, cols), (64 * PITCH, LANES), (CHUNK * PITCH, LANES), (2,) + whole, whole, whole, whole, whole, whole,
        (4,) + whole, window, window, (SLICES,) + window, (SLICES,) + window,
        (9, 18, 8, LANES), (9, 18, 8, LANES), (3, 8, 3, 8, LANES), (8, 9, 8, LANES), (8, 9, 8, LANES),
        (3, BLOCKS + 2, 8, LANES), (2, SLICES, 3, 40, LANES), (3, SLICES, 2, 16, LANES), (3, SLICES, 2, 16, LANES),
        (2, CHUNK, HALO, LANES), (BLOCKS, 16, LANES), (8 * BLOCKS, 4 * LANES),
    ]
    slots = 176
    fine, delta = pl.pallas_call(
        kernel,
        name="parareal",
        out_shape=(jax.ShapeDtypeStruct((rows, cols), F32), jax.ShapeDtypeStruct((8 * BLOCKS, LANES), F32)),
        in_specs=[vmem, vmem, anywhere, anywhere, anywhere],
        out_specs=(anywhere, vmem),
        scratch_shapes=[VMEM(s, F32) for s in shapes]
        + [pltpu.SemaphoreType.DMA((3,)), pltpu.SemaphoreType.DMA((slots,)), pltpu.SemaphoreType.DMA((slots,))],
        compiler_params=pltpu.CompilerParams(vmem_limit_bytes=62 * 2**20, collective_id=0, has_side_effects=True),
    )(jnp.transpose(conv_in, (1, 2, 0)), jnp.transpose(conv_out, (1, 2, 0)), vorticity, stream, forcing)
    grid = 2
    return pl.pallas_call(
        finish_kernel,
        name="finish",
        grid=(grid,),
        out_shape=jax.ShapeDtypeStruct((1, rows, cols), F32),
        in_specs=[
            pl.BlockSpec((rows, cols // grid), lambda i: (0, i)),
            pl.BlockSpec((8 * BLOCKS // grid, LANES), lambda i: (i, 0)),
        ],
        out_specs=pl.BlockSpec((1, rows, cols // grid), lambda i: (0, 0, i)),
    )(fine, delta)


def solution(mesh):
    placed = (P("space", None), P("space", None), P("space", None), P(), P())
    return jax.shard_map(
        body, mesh=mesh, in_specs=placed, out_specs=P("tm", "space", None), check_vma=False
    )
```

profile of v0, /device:TPU:1, one launch (start us, length us, event | category | flops | bytes accessed | tf_op | source)
XLA Modules:
  0.0 87.5 jit_solution(8014783541471756279)
XLA Ops:
  0.0 85.0 %parareal.1 = (f32[32,8192]{1,0:T(8,128)}, f32[128,128]{1,0:T(8,128)}) custom-call(f32[3,3,8]{2,1,0:T(4,128)} %bitcast.2, f32[3,3,8]{2,1,0:T(4,128)} %bitcast.3, f32[32,8192]{1,0:T(8,128)} %vort_hbm.1, f32[32,8192]{1,0:T(8,128)} %stream_hbm.1, f32[32,8192]{1,0:T(8,128)} %force_hbm.1), custom_call_target="tpu_custom_call" | custom-call | tf_op jit(solution)/shard_map/parareal/pallas_call | solution.py:737
  85.0 2.5 %finish.1 = f32[1,32,8192]{2,1,0:T(8,128)} custom-call(f32[32,8192]{1,0:T(8,128)} %get-tuple-element.7.fine, f32[128,128]{1,0:T(8,128)} %get-tuple-element.8.delta), custom_call_target="tpu_custom_call" | custom-call | tf_op jit(solution)/shard_map/finish/pallas_call | solution.py:748
where the time goes:
time: 87.6 us; the launch traced here: 87.5 us
  Pallas kernels  87.5 us (100%)
    pallas_call x1, Pallas kernels, body(): pl.pallas_call(kernel, name='parareal', out_shape=(jax.ShapeDtypeStruct((...  85 us
    pallas_call x1, Pallas kernels, body(): pl.pallas_call(finish_kernel, name='finish', grid=(grid,), out_shape=jax....  2.49 us

commit v1 on v0

--- a/solution.py
+++ b/solution.py
@@ -197,34 +197,32 @@
         fine_stage(one, state, *shared, force.at[0], PAD + 4 * step + 4, 7 - step, of_w[4], of_w[0])
 
 
-def ghosts(ref):
+def ghosts(ref, rows=range(PAD, TALL - PAD, 8)):
     ahead, back = next_chunk(), previous_chunk()
-    for r in range(PAD, TALL - PAD, 8):
+    for r in rows:
         ref[0, r : r + 8, :] = lane_gather(ref[CHUNK, r : r + 8, :], back)
         ref[CHUNK + 1, r : r + 8, :] = lane_gather(ref[1, r : r + 8, :], ahead)
 
 
-def coefficients(stream, forcing, pcoef, qcoef, force):
+def coefficients(stream, forcing, pcoef, qcoef, force, of_stream, of_forcing):
     of_w, of_f = fine_weights()
-    ghosts(stream)
-    count = 9
-    at = [pl.ds(4 + q, 8, stride=count) for q in range(-1, count + 1)]
-
+    ghosts(stream, of_stream)
     group = 4
 
     def body(g, _):
         first = 1 + g * group
         c = pl.ds(first, group)
-        wide = [stream[pl.ds(first - 1, group + 2), a, :] for a in at[1:-1]]
-        x = [stream[c, at[0], :]] + [v[1:-1] for v in wide] + [stream[c, at[-1], :]]
-        for q in range(count):
-            a = at[q + 1]
-            pcoef[c, a, :] = 0.5 - 1.25 * (x[q + 2] - x[q])
-            qcoef[c, a, :] = 0.5 + 1.25 * (wide[q][2:] - wide[q][:-2])
-            f = forcing[c, a, :]
-            force[0, c, a, :] = of_f[0] * f
+        for r in of_stream:
+            rows = slice(r, r + 8)
+            wide = stream[pl.ds(first - 1, group + 2), rows, :]
+            pcoef[c, rows, :] = 0.5 - 1.25 * (stream[c, r + 1 : r + 9, :] - stream[c, r - 1 : r + 7, :])
+            qcoef[c, rows, :] = 0.5 + 1.25 * (wide[2:] - wide[:-2])
+        for r in of_forcing:
+            rows = slice(r, r + 8)
+            f = forcing[c, rows, :]
+            force[0, c, rows, :] = of_f[0] * f
             for k in range(1, 4):
-                force[k, c, a, :] = (of_f[k] / of_w[4]) * f
+                force[k, c, rows, :] = (of_f[k] / of_w[4]) * f
         return 0
 
     lax.fori_loop(0, CHUNK // group, body, 0)
@@ -451,6 +449,7 @@
 
     start[:, REACH - 4 : REACH + 4, :] = rolled[0, mine]
     lay_out(1 - parity)
+    coefficients(fields.at[0], fields.at[1], pcoef, qcoef, force, (32, 40), (24, 32, 40, 48))
 
     recv_all(near)
     win[...] = start[...]
@@ -522,7 +521,9 @@
     for copies in shared:
         for part in range(2):
             recv_all(copies[part])
-    coefficients(fields.at[0], fields.at[1], pcoef, qcoef, force)
+    coefficients(
+        fields.at[0], fields.at[1], pcoef, qcoef, force, (8, 16, 24, 48, 56, 64), (8, 16, 56, 64)
+    )
 
     @pl.when(t == 1)
     def _():

time: 87.6 us -> 86.8 us (level)
  Pallas kernels: 87.5 us -> 86.6 us
where the time goes in v1:
time: 86.8 us; the launch traced here: 86.7 us
  Pallas kernels  86.6 us (100%)
    pallas_call x1, Pallas kernels, body(): pl.pallas_call(kernel, name='parareal', out_shape=(jax.ShapeDtypeStruct((...  84.2 us
    pallas_call x1, Pallas kernels, body(): pl.pallas_call(finish_kernel, name='finish', grid=(grid,), out_shape=jax....  2.49 us

profile of v1, /device:TPU:1, one launch (start us, length us, event | category | flops | bytes accessed | tf_op | source)
XLA Modules:
  0.0 86.7 jit_solution(11879290521720931459)
XLA Ops:
  0.0 84.2 %parareal.1 = (f32[32,8192]{1,0:T(8,128)}, f32[128,128]{1,0:T(8,128)}) custom-call(f32[3,3,8]{2,1,0:T(4,128)} %bitcast.2, f32[3,3,8]{2,1,0:T(4,128)} %bitcast.3, f32[32,8192]{1,0:T(8,128)} %vort_hbm.1, f32[32,8192]{1,0:T(8,128)} %stream_hbm.1, f32[32,8192]{1,0:T(8,128)} %force_hbm.1), custom_call_target="tpu_custom_call" | custom-call | tf_op jit(solution)/shard_map/parareal/pallas_call | solution.py:738
  84.2 2.5 %finish.1 = f32[1,32,8192]{2,1,0:T(8,128)} custom-call(f32[32,8192]{1,0:T(8,128)} %get-tuple-element.7.fine, f32[128,128]{1,0:T(8,128)} %get-tuple-element.8.delta), custom_call_target="tpu_custom_call" | custom-call | tf_op jit(solution)/shard_map/finish/pallas_call | solution.py:749
